TPU v7x, 32 devices: a whole 2x2x4 slice. The times are simulated.
32 devices in a mesh: seq: 8 (over y, x, core), head: 4 (over z).
Axes of the slice: x: 2, y: 2, z: 4, core: 2. Of those that a mesh axis runs over, the one named last changes fastest.
Arguments:
- queries: bfloat16 [4096, 2048], P('seq', 'head'), may hold values from -60 to 60
- keys: bfloat16 [4096, 2048], P('seq', 'head'), may hold values from -6 to 6
- values: bfloat16 [4096, 2048], P('seq', 'head'), may hold values from -6 to 6
- grad_out: bfloat16 [4096, 2048], P('seq', 'head'), may hold values from -6 to 6
- retrieved: int32 [64, 16], P(('seq', 'head')), may hold values from 0 to 63, as said below
- mem_bias: float32 [16], P('head'), may hold values from -2 to 1
Outputs:
- attended: bfloat16 [4096, 2048], P('seq', 'head')
- grad_queries: bfloat16 [4096, 2048], P('seq', 'head')
- grad_keys: bfloat16 [4096, 2048], P('seq', 'head')
- grad_values: bfloat16 [4096, 2048], P('seq', 'head')
Inputs may be any that keep to these rules, and one draw needn't show every extreme that they name: `retrieved`: each row names 16 different blocks. The 8 rows of one segment name exactly 32 distinct blocks together, at most 4 of them from the blocks of any one segment, and exactly 4 from some segment.
All inputs are finite; a program needn't handle non-finite values.
Results may differ from a plain program's by a relative error of at most 0.0055.
Values may be sent and summed in bfloat16 or wider, within the bound.
A program may use at most 128 MiB of HBM per device.

v0:
```python
import math

import jax
import jax.numpy as jnp
from jax import lax
from jax.sharding import PartitionSpec as P

BLK = 64
TOPK = 16
POOL = 32


def product(pattern, former, latter):
    return jnp.einsum(pattern, former, latter, preferred_element_type=jnp.float32)


def attend_group(
    queries, grads, seg_keys, seg_values, mem_keys, mem_values, usable, bias, first_row
):
    row_count, features = queries.shape
    head_count = bias.shape[0]
    head_size = features // head_count
    block_count, top_count, block_len, _ = mem_keys.shape
    seg_len = seg_keys.shape[0]
    score_scale = 1.0 / math.sqrt(head_size)
    query_heads = queries.reshape(block_count, block_len, head_count, head_size)
    grad_heads = grads.reshape(block_count, block_len, head_count, head_size)
    key_heads = seg_keys.reshape(seg_len, head_count, head_size)
    value_heads = seg_values.reshape(seg_len, head_count, head_size)
    mem_key_heads = mem_keys.reshape(block_count, top_count * block_len, head_count, head_size)
    mem_value_heads = mem_values.reshape(block_count, top_count * block_len, head_count, head_size)
    query_pos = first_row + jnp.arange(row_count, dtype=jnp.int32).reshape(
        block_count, 1, block_len, 1
    )
    key_pos = jnp.arange(seg_len, dtype=jnp.int32)
    local_ok = key_pos[None, None, None, :] <= query_pos
    memory_ok = jnp.broadcast_to(usable[:, :, None], (block_count, top_count, block_len)).reshape(
        block_count, 1, 1, top_count * block_len
    )
    local_score = product("nqhd,khd->nhqk", query_heads, key_heads) * score_scale
    local_score = jnp.where(local_ok, local_score, -1e30)
    memory_score = (
        product("nqhd,nkhd->nhqk", query_heads, mem_key_heads) * score_scale
        + bias[None, :, None, None]
    )
    memory_score = jnp.where(memory_ok, memory_score, -1e30)
    highest = jnp.maximum(
        jnp.max(local_score, axis=-1, keepdims=True), jnp.max(memory_score, axis=-1, keepdims=True)
    )
    local_exp = jnp.exp(local_score - highest)
    memory_exp = jnp.exp(memory_score - highest)
    total_mass = jnp.sum(local_exp, axis=-1, keepdims=True) + jnp.sum(
        memory_exp, axis=-1, keepdims=True
    )
    local_prob = local_exp / total_mass
    memory_prob = memory_exp / total_mass
    local_weight = local_prob.astype(jnp.bfloat16)
    memory_weight = memory_prob.astype(jnp.bfloat16)
    attended = product("nhqk,khd->nqhd", local_weight, value_heads) + product(
        "nhqk,nkhd->nqhd", memory_weight, mem_value_heads
    )
    local_dprob = product("nqhd,khd->nhqk", grad_heads, value_heads)
    memory_dprob = product("nqhd,nkhd->nhqk", grad_heads, mem_value_heads)
    row_delta = jnp.sum(local_prob * local_dprob, axis=-1, keepdims=True) + jnp.sum(
        memory_prob * memory_dprob, axis=-1, keepdims=True
    )
    local_dscore = (local_prob * (local_dprob - row_delta) * score_scale).astype(jnp.bfloat16)
    memory_dscore = (memory_prob * (memory_dprob - row_delta) * score_scale).astype(jnp.bfloat16)
    grad_query = product("nhqk,khd->nqhd", local_dscore, key_heads) + product(
        "nhqk,nkhd->nqhd", memory_dscore, mem_key_heads
    )
    local_dkey = product("nhqk,nqhd->khd", local_dscore, query_heads).reshape(seg_len, features)
    local_dvalue = product("nhqk,nqhd->khd", local_weight, grad_heads).reshape(seg_len, features)
    memory_dkey = product("nhqk,nqhd->nkhd", memory_dscore, query_heads).reshape(
        block_count, top_count, block_len, features
    )
    memory_dvalue = product("nhqk,nqhd->nkhd", memory_weight, grad_heads).reshape(
        block_count, top_count, block_len, features
    )
    return (
        attended.reshape(row_count, features).astype(jnp.bfloat16),
        grad_query.reshape(row_count, features).astype(jnp.bfloat16),
        local_dkey,
        local_dvalue,
        memory_dkey,
        memory_dvalue,
    )


def shards(queries, keys, values, grad_out, retrieved, mem_bias):
    seq_count = lax.axis_size("seq")
    position = lax.axis_index("seq")
    seg_len, features = keys.shape
    seg_blocks = seg_len // BLK
    block_total = seq_count * seg_blocks
    capacity = max(2, POOL // seq_count)
    slot_count = seq_count * capacity
    named_blocks = lax.all_gather(retrieved, "head", axis=0, tiled=True)
    flat_named = named_blocks.reshape(-1)
    matches = flat_named[:, None] == jnp.arange(block_total, dtype=jnp.int32)[None, :]
    wanted_flag = jnp.any(matches, axis=0).astype(jnp.int32).reshape(seq_count, seg_blocks)
    rank_within = jnp.cumsum(wanted_flag, axis=1) - 1
    placed = (rank_within[:, :, None] == jnp.arange(capacity, dtype=jnp.int32)[None, None, :]) & (
        wanted_flag[:, :, None] > 0
    )
    request = jnp.sum(
        placed.astype(jnp.int32) * jnp.arange(seg_blocks, dtype=jnp.int32)[None, :, None], axis=1
    )
    slot_table = (jnp.arange(seq_count, dtype=jnp.int32)[:, None] * capacity + rank_within).reshape(
        block_total
    )
    slot_of = jnp.sum(jnp.where(matches, slot_table[None, :], 0), axis=1).reshape(seg_blocks, TOPK)
    tables = lax.all_gather(request, "seq", axis=0, tiled=True).reshape(
        seq_count, seq_count, capacity
    )
    asked_blocks = lax.dynamic_index_in_dim(tables, position, 1, keepdims=False)
    served_blocks = asked_blocks.reshape(slot_count)
    key_blocks = keys.reshape(seg_blocks, BLK, features)
    value_blocks = values.reshape(seg_blocks, BLK, features)
    tile_keys, tile_values = (
        lax.all_to_all(key_blocks[served_blocks], "seq", split_axis=0, concat_axis=0, tiled=True),
        lax.all_to_all(value_blocks[served_blocks], "seq", split_axis=0, concat_axis=0, tiled=True),
    )
    block_index = position * seg_blocks + jnp.arange(seg_blocks, dtype=jnp.int32)
    usable = named_blocks < block_index[:, None]
    group_rows = min(512, seg_len)
    group_blocks = group_rows // BLK
    group_count = seg_len // group_rows

    def step(state_carry, group_index):
        key_grad, value_grad, tile_kgrad, tile_vgrad = state_carry
        row_start = group_index * group_rows
        slot_rows = slot_of.reshape(-1)
        mem_keys = tile_keys[slot_rows].reshape(group_blocks, TOPK, BLK, features)
        mem_values = tile_values[slot_rows].reshape(group_blocks, TOPK, BLK, features)
        results = attend_group(
            queries, grad_out, keys, values, mem_keys, mem_values, usable, mem_bias, row_start
        )
        key_grad = key_grad + results[2]
        value_grad = value_grad + results[3]
        tile_kgrad = tile_kgrad.at[slot_rows].add(
            results[4].reshape(group_blocks * TOPK, BLK, features)
        )
        tile_vgrad = tile_vgrad.at[slot_rows].add(
            results[5].reshape(group_blocks * TOPK, BLK, features)
        )
        return ((key_grad, value_grad, tile_kgrad, tile_vgrad), (results[0], results[1]))

    zero_local = jnp.zeros((seg_len, features), jnp.float32)
    zero_tiles = jnp.zeros((slot_count, BLK, features), jnp.float32)
    finals, outputs = lax.scan(
        step,
        (zero_local, zero_local, zero_tiles, zero_tiles),
        jnp.arange(group_count, dtype=jnp.int32),
    )
    back_keys, back_values = (
        lax.all_to_all(
            finals[2].astype(jnp.bfloat16), "seq", split_axis=0, concat_axis=0, tiled=True
        ),
        lax.all_to_all(
            finals[3].astype(jnp.bfloat16), "seq", split_axis=0, concat_axis=0, tiled=True
        ),
    )
    key_total = (
        finals[0]
        .reshape(seg_blocks, BLK, features)
        .at[served_blocks]
        .add(back_keys.astype(jnp.float32))
    )
    value_total = (
        finals[1]
        .reshape(seg_blocks, BLK, features)
        .at[served_blocks]
        .add(back_values.astype(jnp.float32))
    )
    attended = outputs[0].reshape(seg_len, features)
    grad_queries = outputs[1].reshape(seg_len, features)
    return (
        attended,
        grad_queries,
        key_total.reshape(seg_len, features).astype(jnp.bfloat16),
        value_total.reshape(seg_len, features).astype(jnp.bfloat16),
    )


def solution(mesh):
    placed = (
        P("seq", "head"),
        P("seq", "head"),
        P("seq", "head"),
        P("seq", "head"),
        P(("seq", "head"), None),
        P("head"),
    )
    return jax.shard_map(
        shards,
        mesh=mesh,
        in_specs=placed,
        out_specs=(P("seq", "head"), P("seq", "head"), P("seq", "head"), P("seq", "head")),
        check_vma=False,
    )
```

profile of v0, /device:TPU:0, one launch (start us, length us, event | category | flops | bytes accessed | tf_op | source)
XLA Modules:
  0.0 361.5 jit_solution(16766139127247901351)
XLA Ops:
  0.6 12.8 %all-gather = s32[4,2,16]{2,1,0:T(2,128)S(1)} all-gather(s32[1,2,16]{2,1,0:T(2,128)} %bitcast.138), channel_id=1, replica_groups=mesh['seq'=8,'head'=4] {'head'}, dimensions={0}, use_global_device_ids=true | all-gather | bytes 640 | tf_op jit(solution)/shard_map/all_gather | solution.py:98
  14.2 8.9 %all-gather.1 = s32[8,8,4]{1,2,0:T(4,128)S(1)} all-gather(s32[1,8,4]{1,2,0:T(4,128)S(1)} %bitcast.137), channel_id=1, replica_groups=mesh['seq'=8,'head'=4] {'seq'}, dimensions={0}, use_global_device_ids=true | all-gather | bytes 1152 | tf_op jit(solution)/shard_map/all_gather | solution.py:113
  49.3 7.6 %all-to-all-done = bf16[32,64,512]{2,1,0:T(8,128)(2,1)S(1)} async-done(((bf16[32,64,512]{2,1,0:T(8,128)(2,1)}), bf16[32,64,512]{2,1,0:T(8,128)(2,1)S(1)}, u32[]{:S(2)}, u32[]{:S(2)}) %all-to-all-start) | async-done | bytes 2097184 | tf_op jit(solution)/shard_map/all_to_all | solution.py:121
  56.9 4.5 %all-to-all-start.1 = ((bf16[32,64,512]{2,1,0:T(8,128)(2,1)}), bf16[32,64,512]{2,1,0:T(8,128)(2,1)}, u32[]{:S(2)}, u32[]{:S(2)}) async-start(bf16[32,64,512]{2,1,0:T(8,128)(2,1)} %gather_fusion.2), calls=%async_computation.1 | async-start | bytes 4194304 | tf_op jit(solution)/shard_map/all_to_all | solution.py:122
  61.4 6.6 %gather_fusion.1 = bf16[128,64,512]{2,1,0:T(8,128)(2,1)} fusion(bf16[32,64,512]{2,1,0:T(8,128)(2,1)S(1)} %all-to-all-done, s32[1024]{0:T(1024)S(1)} %pad_clamp_fusion), kind=kCustom, calls=%fused_computation.1 | custom fusion | bytes 16777728 | tf_op jit(solution)/shard_map/while/body/eval_jaxpr/gather | solution.py:134
  68.0 12.6 %reshape.223 = bf16[8,1024,4,128]{3,2,1,0:T(4,128)(2,1)} reshape(bf16[128,64,512]{2,1,0:T(8,128)(2,1)} %gather_fusion.1) | data formatting | bytes 16777216 | tf_op jit(solution)/shard_map/while/body/eval_jaxpr/reshape;while/body/eval_jaxpr/reshape | solution.py:30
  80.6 9.8 %bitcast_reduce_fusion = (f32[8,4,64]{2,1,0:T(4,128)S(1)}, f32[8,4,1024,64]{2,3,1,0:T(8,128)}) fusion(f32[4]{0:T(128)S(1)} %copy-done.19, pred[8,1024]{1,0:T(8,128)(4,1)S(1)} %broadcast_in_dim.99, bf16[8,64,4,128]{3,2,1,0:T(4,128)(2,1)S(1)} %copy-done.14, bf16[8,1024,4,128]{3,2,1,0:T(4,128)(2,1)} %reshape.223), kind=kOutput, calls=%fused_computation.17 | convolution fusion | flops 545257472 | bytes 17317904 | tf_op jit(solution)/shard_map/while/body/eval_jaxpr/nqhd,nkhd->nhqk/dot_general | solution.py:14
  91.9 4.6 %fusion.14 = f32[8,4,64]{2,1,0:T(4,128)S(1)} fusion(f32[8,4,1024,64]{2,3,1,0:T(8,128)} %get-tuple-element.41, f32[8,4,64]{2,1,0:T(4,128)S(1)} %copy.116, f32[4]{0:T(128)S(1)} %copy-done.19, pred[8,1024]{1,0:T(8,128)(4,1)S(1)} %broadcast_in_dim.99), kind=kLoop, calls=%fused_computation.29 | loop fusion | flops 10483712 | bytes 8413200 | tf_op jit(solution)/shard_map/while/body/eval_jaxpr/reduce_sum | solution.py:52
  99.1 8.1 %gather_fusion.3 = bf16[128,64,512]{2,1,0:T(8,128)(2,1)} fusion(bf16[32,64,512]{2,1,0:T(8,128)(2,1)} %all-to-all-done.1, s32[1024]{0:T(1024)S(1)} %pad_clamp_fusion), kind=kCustom, calls=%fused_computation.3 | custom fusion | bytes 16777728 | tf_op jit(solution)/shard_map/while/body/eval_jaxpr/gather | solution.py:135
  107.3 12.6 %reshape.226 = bf16[8,1024,4,128]{3,2,1,0:T(4,128)(2,1)} reshape(bf16[128,64,512]{2,1,0:T(8,128)(2,1)} %gather_fusion.3) | data formatting | bytes 16777216 | tf_op jit(solution)/shard_map/while/body/eval_jaxpr/reshape;while/body/eval_jaxpr/reshape | solution.py:31
  119.9 10.4 %fusion = (f32[8,4,64]{2,1,0:T(4,128)S(1)}, f32[8,4,1024,64]{2,3,1,0:T(8,128)}) fusion(f32[8,4,64]{2,1,0:T(4,128)S(1)} %copy.119, f32[8,4,64]{2,1,0:T(4,128)S(1)} %copy.116, f32[4]{0:T(128)S(1)} %copy-done.19, f32[8,4,1024,64]{2,3,1,0:T(8,128)} %get-tuple-element.41, pred[8,1024]{1,0:T(8,128)(4,1)S(1)} %broadcast_in_dim.99, ...), kind=kOutput, calls=%fused_computation.12 | convolution fusion | flops 551548928 | bytes 25722896 | tf_op jit(solution)/shard_map/while/body/eval_jaxpr/nqhd,nkhd->nhqk/dot_general | solution.py:14
  137.0 6.9 %fusion.3 = (bf16[8,4,64,1024]{3,2,1,0:T(8,128)(2,1)S(1)}, bf16[8,4,64,1024]{3,2,1,0:T(8,128)(2,1)}) fusion(f32[8,4,1024,64]{2,3,1,0:T(8,128)S(1)} %copy-done.10, f32[8,4,64]{2,1,0:T(4,128)S(1)} %copy.129, f32[8,4,64]{2,1,0:T(4,128)S(1)} %copy.119, f32[8,4,64]{2,1,0:T(4,128)S(1)} %copy.116, f32[4]{0:T(128)S(1)} %copy-done.19, ...), kind=kLoop, calls=%fused_computation.15 | loop fusion | flops 20971520 | bytes 25198608 | tf_op jit(solution)/shard_map/while/body/eval_jaxpr/convert_element_type | solution.py:68
  146.4 12.3 %copy.136 = f32[8,1024,4,128]{3,2,1,0:T(4,128)} copy(f32[8,1024,4,128]{3,1,2,0:T(8,128)S(1)} %convolution_bitcast_fusion.1) | data formatting | bytes 33554432 | tf_op jit(solution)/shard_map/while/body/eval_jaxpr/nhqk,nqhd->nkhd/transpose | solution.py:14
  158.7 19.9 %reshape.269 = f32[128,64,512]{2,1,0:T(8,128)} reshape(f32[8,1024,4,128]{3,2,1,0:T(4,128)} %copy.136) | data formatting | bytes 33554432 | tf_op jit(solution)/shard_map/while/body/eval_jaxpr/reshape;while/body/eval_jaxpr/reshape | solution.py:142
  181.0 38.9 %scatter_fusion = f32[32,64,512]{2,1,0:T(8,128)} fusion(f32[32,64,512]{2,1,0:T(8,128)} %broadcast_in_dim.104.clone, s32[128]{0:T(128)S(1)} %fusion.51, f32[128,64,512]{2,1,0:T(8,128)} %reshape.269), kind=kCustom, calls=%fused_computation.4 | custom fusion | flops 4194304 | bytes 50332160 | tf_op jit(solution)/shard_map/while/body/eval_jaxpr/scatter-add | solution.py:141
  223.7 4.7 %all-to-all-start.2 = ((bf16[32,64,512]{2,1,0:T(8,128)(2,1)}), bf16[32,64,512]{2,1,0:T(8,128)(2,1)}, u32[]{:S(2)}, u32[]{:S(2)}) async-start(bf16[32,64,512]{2,1,0:T(8,128)(2,1)} %convert_element_type.79), calls=%async_computation.2 | async-start | bytes 4194304 | tf_op jit(solution)/shard_map/all_to_all | solution.py:157
  228.5 6.3 %fusion.25 = f32[8,64,4,128]{3,1,0,2:T(8,128)S(1)} fusion(bf16[8,1024,4,128]{3,2,1,0:T(4,128)(2,1)} %reshape.223, bf16[8,4,64,1024]{3,2,1,0:T(8,128)(2,1)} %copy-done.9), kind=kOutput, calls=%fused_computation.44 | convolution fusion | flops 536870912 | bytes 13631488 | tf_op jit(solution)/shard_map/while/body/eval_jaxpr/nhqk,nkhd->nqhd/dot_general | solution.py:14
  239.8 12.3 %copy.140 = f32[8,1024,4,128]{3,2,1,0:T(4,128)} copy(f32[8,1024,4,128]{3,1,2,0:T(8,128)S(1)} %convolution_bitcast_fusion) | data formatting | bytes 33554432 | tf_op jit(solution)/shard_map/while/body/eval_jaxpr/nhqk,nqhd->nkhd/transpose | solution.py:14
  252.0 19.9 %reshape.285 = f32[128,64,512]{2,1,0:T(8,128)} reshape(f32[8,1024,4,128]{3,2,1,0:T(4,128)} %copy.140) | data formatting | bytes 33554432 | tf_op jit(solution)/shard_map/while/body/eval_jaxpr/reshape;while/body/eval_jaxpr/reshape | solution.py:145
  274.4 38.8 %scatter_fusion.2 = f32[32,64,512]{2,1,0:T(8,128)} fusion(f32[32,64,512]{2,1,0:T(8,128)} %broadcast_in_dim.104.clone.1, s32[128]{0:T(128)S(1)} %fusion.51, f32[128,64,512]{2,1,0:T(8,128)} %reshape.285), kind=kCustom, calls=%fused_computation.6 | custom fusion | flops 4194304 | bytes 50332160 | tf_op jit(solution)/shard_map/while/body/eval_jaxpr/scatter-add | solution.py:144
  317.0 4.5 %all-to-all-start.3 = ((bf16[32,64,512]{2,1,0:T(8,128)(2,1)}), bf16[32,64,512]{2,1,0:T(8,128)(2,1)}, u32[]{:S(2)}, u32[]{:S(2)}) async-start(bf16[32,64,512]{2,1,0:T(8,128)(2,1)} %convert_element_type.83), calls=%async_computation.3 | async-start | bytes 4194304 | tf_op jit(solution)/shard_map/all_to_all | solution.py:160
  321.6 6.4 %fusion.20 = f32[8,64,4,128]{3,1,0,2:T(8,128)S(1)} fusion(bf16[8,1024,4,128]{3,2,1,0:T(4,128)(2,1)} %reshape.226, bf16[8,4,64,1024]{3,2,1,0:T(8,128)(2,1)} %get-tuple-element.37), kind=kOutput, calls=%fused_computation.43 | convolution fusion | flops 536870912 | bytes 13631488 | tf_op jit(solution)/shard_map/while/body/eval_jaxpr/nhqk,nkhd->nqhd/dot_general | solution.py:14
  342.6 6.5 %scatter_fusion.1 = f32[8,64,512]{2,1,0:T(8,128)S(1)} fusion(f32[8,64,512]{2,1,0:T(8,128)S(1)} %reshape.228, s32[32]{0:T(128)S(1)} %copy-done.18, f32[32,64,512]{2,1,0:T(8,128)} %convert_element_type.80), kind=kCustom, calls=%fused_computation.5 | custom fusion | flops 1048576 | bytes 12583040 | tf_op jit(solution)/shard_map/scatter-add | solution.py:168
  354.0 6.5 %scatter_fusion.3 = f32[8,64,512]{2,1,0:T(8,128)S(1)} fusion(f32[8,64,512]{2,1,0:T(8,128)S(1)} %reshape.230, s32[32]{0:T(128)S(1)} %copy-done.18, f32[32,64,512]{2,1,0:T(8,128)} %convert_element_type.84), kind=kCustom, calls=%fused_computation.7 | custom fusion | flops 1048576 | bytes 12583040 | tf_op jit(solution)/shard_map/scatter-add | solution.py:174
  (109 shorter events, 77.9 us)
Async XLA Ops:
  23.5 3.1 copy-start.17
  23.5 6.8 %copy-start.6 = (bf16[512,512]{1,0:T(8,128)(2,1)S(1)}, bf16[512,512]{1,0:T(8,128)(2,1)}, u32[]{:S(2)}) copy-start(bf16[512,512]{1,0:T(8,128)(2,1)} %param.7) | copy-start | bytes 1572868
  26.6 10.9 %copy-start.7 = (bf16[512,512]{1,0:T(8,128)(2,1)S(1)}, bf16[512,512]{1,0:T(8,128)(2,1)}, u32[]{:S(2)}) copy-start(bf16[512,512]{1,0:T(8,128)(2,1)} %param.8) | copy-start | bytes 1572868
  26.6 30.3 %all-to-all-start = ((bf16[32,64,512]{2,1,0:T(8,128)(2,1)}), bf16[32,64,512]{2,1,0:T(8,128)(2,1)S(1)}, u32[]{:S(2)}, u32[]{:S(2)}) async-start(bf16[32,64,512]{2,1,0:T(8,128)(2,1)} %gather_fusion), calls=%async_computation | async-start | bytes 4194304 | tf_op jit(solution)/shard_map/all_to_all | solution.py:121
  43.7 1.9 copy-start
  56.9 42.2 %all-to-all-start.1 = ((bf16[32,64,512]{2,1,0:T(8,128)(2,1)}), bf16[32,64,512]{2,1,0:T(8,128)(2,1)}, u32[]{:S(2)}, u32[]{:S(2)}) async-start(bf16[32,64,512]{2,1,0:T(8,128)(2,1)} %gather_fusion.2), calls=%async_computation.1 | async-start | bytes 4194304 | tf_op jit(solution)/shard_map/all_to_all | solution.py:122
  68.0 12.6 %copy-start.14 = (bf16[8,64,4,128]{3,2,1,0:T(4,128)(2,1)S(1)}, bf16[8,64,4,128]{3,2,1,0:T(4,128)(2,1)}, u32[]{:S(2)}) copy-start(bf16[8,64,4,128]{3,2,1,0:T(4,128)(2,1)} %reshape.219) | copy-start | bytes 1572868
  68.0 12.6 %copy-start.19 = (f32[4]{0:T(128)S(1)}, f32[4]{0:T(128)}, u32[]{:S(2)}) copy-start(f32[4]{0:T(128)} %param.11) | copy-start | bytes 52
  80.6 9.8 %copy-start.1 = (f32[4,512,512]{1,2,0:S(1)}, f32[4,512,512]{1,2,0}, u32[]{:S(2)}) copy-start(f32[4,512,512]{1,2,0} %copy-done) | copy-start | bytes 12582916
  107.3 12.6 %copy-start.13 = (bf16[8,64,4,128]{3,2,1,0:T(4,128)(2,1)S(1)}, bf16[8,64,4,128]{3,2,1,0:T(4,128)(2,1)}, u32[]{:S(2)}) copy-start(bf16[8,64,4,128]{3,2,1,0:T(4,128)(2,1)} %reshape.227) | copy-start | bytes 1572868
  119.8 10.4 %copy-start.3 = (f32[8,4,64,512]{3,2,0,1:T(8,128)S(1)}, f32[8,4,64,512]{3,2,0,1:T(8,128)}, u32[]{:S(2)}) copy-start(f32[8,4,64,512]{3,2,0,1:T(8,128)} %fusion.17) | copy-start | bytes 12582916
  119.9 10.8 %copy-start.5 = (f32[4,512,512]{1,2,0:S(1)}, f32[4,512,512]{1,2,0}, u32[]{:S(2)}) copy-start(f32[4,512,512]{1,2,0} %fusion.36) | copy-start | bytes 12582916
  130.6 2.2 copy-start.2
  132.8 4.1 %copy-start.10 = (f32[8,4,1024,64]{2,3,1,0:T(8,128)S(1)}, f32[8,4,1024,64]{2,3,1,0:T(8,128)}, u32[]{:S(2)}) copy-start(f32[8,4,1024,64]{2,3,1,0:T(8,128)} %get-tuple-element.43) | copy-start | bytes 25165828
  143.9 2.5 copy-start.9
  223.7 93.3 %all-to-all-start.2 = ((bf16[32,64,512]{2,1,0:T(8,128)(2,1)}), bf16[32,64,512]{2,1,0:T(8,128)(2,1)}, u32[]{:S(2)}, u32[]{:S(2)}) async-start(bf16[32,64,512]{2,1,0:T(8,128)(2,1)} %convert_element_type.79), calls=%async_computation.2 | async-start | bytes 4194304 | tf_op jit(solution)/shard_map/all_to_all | solution.py:157
  228.5 6.4 %copy-start.11 = (bf16[8,4,64,512]{3,2,0,1:T(8,128)(2,1)S(1)}, bf16[8,4,64,512]{3,2,0,1:T(8,128)(2,1)}, u32[]{:S(2)}) copy-start(bf16[8,4,64,512]{3,2,0,1:T(8,128)(2,1)} %multiply_convert_fusion) | copy-start | bytes 6291460
  228.5 6.4 %copy-start.16 = (bf16[512,4,128]{2,1,0:T(4,128)(2,1)S(1)}, bf16[512,4,128]{2,1,0:T(4,128)(2,1)}, u32[]{:S(2)}) copy-start(bf16[512,4,128]{2,1,0:T(4,128)(2,1)} %reshape.218) | copy-start | bytes 1572868
  234.9 2.4 copy-start.8
  317.0 32.9 %all-to-all-start.3 = ((bf16[32,64,512]{2,1,0:T(8,128)(2,1)}), bf16[32,64,512]{2,1,0:T(8,128)(2,1)}, u32[]{:S(2)}, u32[]{:S(2)}) async-start(bf16[32,64,512]{2,1,0:T(8,128)(2,1)} %convert_element_type.83), calls=%async_computation.3 | async-start | bytes 4194304 | tf_op jit(solution)/shard_map/all_to_all | solution.py:160
  321.6 6.4 %copy-start.4 = (f32[8,4,64,512]{3,2,0,1:T(8,128)S(1)}, f32[8,4,64,512]{3,2,0,1:T(8,128)}, u32[]{:S(2)}) copy-start(f32[8,4,64,512]{3,2,0,1:T(8,128)} %fusion.17) | copy-start | bytes 12582916
  321.6 6.4 %copy-start.15 = (bf16[512,4,128]{2,1,0:T(4,128)(2,1)S(1)}, bf16[512,4,128]{2,1,0:T(4,128)(2,1)}, u32[]{:S(2)}) copy-start(bf16[512,4,128]{2,1,0:T(4,128)(2,1)} %reshape.224) | copy-start | bytes 1572868
  328.0 2.0 copy-start.12
  336.2 6.4 %copy-start.18 = (s32[32]{0:T(128)S(1)}, s32[32]{0:T(128)}, u32[]{:S(2)}) copy-start(s32[32]{0:T(128)} %copy-done.17) | copy-start | bytes 388
where the time goes:
time: 368 us; the launch traced here: 361 us
  local copies, waits for them, and re-layouts  137 us (37%)
  other arithmetic  129 us (35%)
  matrix products  47.7 us (13%)
  blocking collectives  21.8 us (6%)
  starting transfers between devices  17.6 us (5%)
  waiting for transfers between devices  7.64 us (2%)
    dot_general x10, matrix products, product(): jnp.einsum(pattern, former, latter, preferred_element_type=jnp.float32)  43.3 us
    scatter-add x1, other arithmetic, step(): tile_kgrad.at[slot_rows]  38.9 us
    scatter-add x1, other arithmetic, step(): tile_vgrad.at[slot_rows]  38.8 us
    transpose x4, local copies, waits for them, and re-layouts, product(): jnp.einsum(pattern, former, latter, preferred_element_type=jnp.float32)  25.9 us
    reshape x1, local copies, waits for them, and re-layouts, step(): results[4].reshape(group_blocks * TOPK, BLK, features)  19.9 us
    reshape x1, local copies, waits for them, and re-layouts, step(): results[5].reshape(group_blocks * TOPK, BLK, features)  19.9 us
    all_gather x1, blocking collectives, shards(): named_blocks = lax.all_gather(retrieved, 'head', axis=0, tiled=True)  12.8 us
    reshape x1, local copies, waits for them, and re-layouts, attend_group(): mem_values.reshape(block_count, top_count * block_len, head_count, head_s...  12.6 us
  transfers between devices with their start and end apart: 4, of which 1 were waited for; matrix products, arithmetic and copies ran while one was open for 47% of the time, Pallas kernels for 0%

commit v1 on v0

v1 whole, which is shorter than its diff:
```python
import functools
import math

import jax
import jax.numpy as jnp
from jax import lax
from jax.experimental import pallas as pl
from jax.experimental.pallas import tpu as pltpu
from jax.sharding import PartitionSpec as P

BLK = 64
LOG2E = math.log2(math.e)
NEG = -1e30
MESH = pl.DeviceIdType.MESH
F32 = jnp.float32
BF16 = jnp.bfloat16


def matmul(left, right):
    return jnp.dot(left, right, preferred_element_type=F32)


def owner_core(segment):
    return lax.rem((segment + 1) // 2, 2)


def fused(
    dims,
    table_in,
    bias_ref,
    q_ref,
    k_ref,
    v_ref,
    g_ref,
    o_ref,
    dq_ref,
    dk_ref,
    dv_ref,
    table,
    q_buf,
    g_buf,
    k_buf,
    v_buf,
    kt_buf,
    vt_buf,
    dk_acc,
    dv_acc,
    part,
    stage,
    bias_rows,
    qt,
    gt,
    ot,
    dqt,
    stat,
    hop1_send,
    hop1_recv,
    hop2_send,
    hop2_recv,
    in_send,
    in_recv,
    fwd_send,
    fwd_recv,
    part_send,
    part_recv,
    out_send,
    out_recv,
):
    seq_count, head_dev, chips, seg_len, hd, rows_dev, top = dims
    seg_blocks = seg_len // BLK
    scale = 1.0 / math.sqrt(hd)
    me = lax.axis_index("seq")
    zed = lax.axis_index("head")
    chip = me // 2
    core = lax.rem(me, 2)
    sibling = chip * 2 + 1 - core

    barrier = pltpu.get_barrier_semaphore()
    for j in range(1, seq_count):
        pl.semaphore_signal(
            barrier, inc=1, device_id={"seq": lax.rem(me + j, seq_count)}, device_id_type=MESH
        )
    for j in range(1, head_dev):
        pl.semaphore_signal(
            barrier, inc=1, device_id={"head": lax.rem(zed + j, head_dev)}, device_id_type=MESH
        )
    pl.semaphore_wait(barrier, seq_count + head_dev - 2)

    def hop1(j):
        return pltpu.make_async_remote_copy(
            src_ref=table_in,
            dst_ref=table.at[me, zed],
            send_sem=hop1_send.at[j - 1],
            recv_sem=hop1_recv.at[j - 1],
            device_id={"head": lax.rem(zed + j, head_dev)},
            device_id_type=MESH,
        )

    for j in range(1, head_dev):
        hop1(j).start()
    table[me, zed] = table_in[...]

    arrays = ((k_ref, k_buf), (q_ref, q_buf), (v_ref, v_buf), (g_ref, g_buf))
    goes_to = owner_core(me)

    def push(a, j):
        src, buf = arrays[a]
        target_chip = lax.rem(chip + 1 + j, chips)
        columns = pl.ds(pl.multiple_of(target_chip * hd, hd), hd)
        slot = me if a in (0, 2) else chip
        return (
            src.at[:, columns],
            buf.at[slot],
            target_chip * 2 + goes_to,
            in_send.at[a, j],
            in_recv.at[a, chip],
        )

    def push_remote(a, j):
        src, dst, device, send, recv = push(a, j)
        return pltpu.make_async_remote_copy(
            src_ref=src,
            dst_ref=dst,
            send_sem=send,
            recv_sem=recv,
            device_id={"seq": device},
            device_id_type=MESH,
        )

    for a in range(4):
        for j in range(chips - 1):
            push_remote(a, j).start()

        @pl.when(goes_to != core)
        def _():
            push_remote(a, chips - 1).start()

        @pl.when(goes_to == core)
        def _():
            src, dst, _, _, recv = push(a, chips - 1)
            pltpu.make_async_copy(src, dst, recv).start()

    for j in range(1, head_dev):
        hop1(j).wait()

    def hop2(j):
        return pltpu.make_async_remote_copy(
            src_ref=table.at[me],
            dst_ref=table.at[me],
            send_sem=hop2_send.at[j - 1],
            recv_sem=hop2_recv.at[j - 1],
            device_id={"seq": lax.rem(me + j, seq_count)},
            device_id_type=MESH,
        )

    for j in range(1, seq_count):
        hop2(j).start()

    dk_acc[...] = jnp.zeros_like(dk_acc)
    dv_acc[...] = jnp.zeros_like(dv_acc)

    def segment_of(pair, which):
        return pair * 2 + lax.rem(pair + which, 2)

    def in_wait(a, pair):
        _, buf = arrays[a]
        slot = segment_of(pair, core) if a in (0, 2) else pair
        pltpu.make_async_copy(buf.at[slot], buf.at[slot], in_recv.at[a, pair]).wait()

    def forward(a, pair, which):
        buf = k_buf if a == 0 else v_buf
        spot = buf.at[segment_of(pair, which)]
        return pltpu.make_async_remote_copy(
            src_ref=spot,
            dst_ref=spot,
            send_sem=fwd_send.at[a, pair],
            recv_sem=fwd_recv.at[a, pair],
            device_id={"seq": sibling},
            device_id_type=MESH,
        )

    for kind in range(2):
        for pair in range(chips):
            in_wait(2 * kind, pair)
            forward(kind, pair, core).start()
            in_wait(2 * kind + 1, pair)
    for j in range(1, seq_count):
        hop2(j).wait()
    for pair in range(chips):
        for kind, buf, turned in ((0, k_buf, kt_buf), (1, v_buf, vt_buf)):
            mine = segment_of(pair, core)
            turned[mine] = buf[mine].T
            forward(kind, pair, 1 - core).wait_recv()
            other = segment_of(pair, 1 - core)
            turned[other] = buf[other].T
            forward(kind, pair, core).wait_send()

    bias2 = bias_ref[0, chip]
    both2 = bias_ref[1, chip]
    score2 = scale * LOG2E
    kb_seg = (seg_blocks, 1, seg_len)
    tile = (seg_blocks, BLK, seg_len)

    def scores(k, rows):
        raw = matmul(k_buf[k], qt[...]).reshape(tile)
        return raw * score2 + rows.reshape(kb_seg)

    def triangle(value):
        key = lax.broadcasted_iota(jnp.int32, (seg_len, seg_len), 0)
        query = lax.broadcasted_iota(jnp.int32, (seg_len, seg_len), 1)
        return jnp.where((key <= query).reshape(tile), value, NEG)

    def rows_of(k):
        return bias_rows[pl.ds(pl.multiple_of(k * seg_blocks, seg_blocks), seg_blocks), :]

    def out_send_copy(a, pair, seg):
        ref = (o_ref, dq_ref, dk_ref, dv_ref)[a]
        return pltpu.make_async_remote_copy(
            src_ref=stage.at[a, pair],
            dst_ref=ref.at[:, pl.ds(pl.multiple_of(chip * hd, hd), hd)],
            send_sem=out_send.at[a, pair],
            recv_sem=out_recv.at[a, chip],
            device_id={"seq": seg},
            device_id_type=MESH,
        )

    def emit(a, pair, seg):
        @pl.when(seg != me)
        def _():
            out_send_copy(a, pair, seg).start()

        @pl.when(seg == me)
        def _():
            ref = (o_ref, dq_ref, dk_ref, dv_ref)[a]
            pltpu.make_async_copy(
                stage.at[a, pair],
                ref.at[:, pl.ds(pl.multiple_of(chip * hd, hd), hd)],
                out_recv.at[a, chip],
            ).start()

    def part_copy(kind, pair, which):
        acc = dk_acc if kind == 0 else dv_acc
        return pltpu.make_async_remote_copy(
            src_ref=acc.at[segment_of(pair, which)],
            dst_ref=part.at[kind, pair],
            send_sem=part_send.at[kind, pair],
            recv_sem=part_recv.at[kind, pair],
            device_id={"seq": sibling},
            device_id_type=MESH,
        )

    def each_segment(step, carry):
        pair = chips - 1 - step
        seg = segment_of(pair, core)
        lists = table[seg].reshape(head_dev * 8, 128).astype(BF16)
        slot = lax.broadcasted_iota(jnp.int32, (head_dev * 8, seg_len), 0)
        lane_block = lax.broadcasted_iota(jnp.int32, (head_dev * 8, seg_len), 1) // BLK
        at_block = (slot // 8) * rows_dev + lax.rem(slot, 8)
        pick = jnp.where((lax.rem(slot, 8) < rows_dev) & (at_block == lane_block), 1.0, 0.0)
        named_of = lax.dot_general(
            lists, pick.astype(BF16), (((0,), (0,)), ((), ())), preferred_element_type=F32
        )
        kb = lax.broadcasted_iota(jnp.int32, (seq_count * seg_blocks, seg_len), 0)
        block = (
            seg * seg_blocks
            + lax.broadcasted_iota(jnp.int32, (seq_count * seg_blocks, seg_len), 1) // BLK
        )
        kb_f = kb.astype(F32)
        named = named_of[0:1, :] == kb_f
        for t in range(1, top):
            named = named | (named_of[t : t + 1, :] == kb_f)
        same = kb >= seg * seg_blocks
        before = jnp.where(
            same, jnp.where(named, both2, 0.0), jnp.where(named, bias2, NEG)
        )
        bias_rows[...] = jnp.where(kb < block, before, jnp.where(kb == block, 0.0, NEG))

        qt[...] = q_buf[pair].T
        gt[...] = g_buf[pair].T

        first = triangle(scores(seg, rows_of(seg)))
        top_row = jnp.max(jnp.max(first, axis=0), axis=0, keepdims=True)
        weight = jnp.exp2(first - top_row.reshape(1, 1, seg_len))
        stat[0:1, :] = top_row
        stat[1:2, :] = jnp.sum(jnp.sum(weight, axis=0), axis=0, keepdims=True)
        ot[...] = matmul(vt_buf[seg], weight.reshape(seg_len, seg_len).astype(BF16))

        def forward_tile(k, c):
            value = scores(k, rows_of(k))
            old = stat[0:1, :]
            new = jnp.maximum(old, jnp.max(jnp.max(value, axis=0), axis=0, keepdims=True))
            shrink = jnp.exp2(old - new)
            weight = jnp.exp2(value - new.reshape(1, 1, seg_len))
            stat[0:1, :] = new
            stat[1:2, :] = stat[1:2, :] * shrink + jnp.sum(
                jnp.sum(weight, axis=0), axis=0, keepdims=True
            )
            ot[...] = ot[...] * shrink + matmul(
                vt_buf[k], weight.reshape(seg_len, seg_len).astype(BF16)
            )
            return c

        lax.fori_loop(0, seg, forward_tile, 0)
        mass = stat[1:2, :]
        ot[...] = ot[...] / mass
        stage[0, pair] = ot[...].T.astype(BF16)
        emit(0, pair, seg)
        lse = stat[0:1, :] + jnp.log2(mass)
        stat[2:3, :] = jnp.sum(ot[...] * gt[...].astype(F32), axis=0, keepdims=True)
        stat[3:4, :] = lse
        dqt[...] = jnp.zeros_like(dqt)

        def backward_tile(k, diagonal):
            value = scores(k, rows_of(k) - stat[3:4, :])
            if diagonal:
                value = triangle(value)
            prob = jnp.exp2(value).reshape(seg_len, seg_len)
            dprob = matmul(v_buf[k], gt[...])
            dscore = (prob * (dprob - stat[2:3, :])).astype(BF16)
            dv_acc[k] += matmul(prob.astype(BF16), g_buf[pair])
            dk_acc[k] += matmul(dscore, q_buf[pair])
            dqt[...] += matmul(kt_buf[k], dscore)

        backward_tile(seg, True)

        def backward_step(k, c):
            backward_tile(k, False)
            return c

        lax.fori_loop(0, seg, backward_step, 0)
        part_copy(0, pair, 1 - core).start()
        part_copy(1, pair, 1 - core).start()
        stage[1, pair] = (dqt[...] * scale).T.astype(BF16)
        emit(1, pair, seg)
        part_copy(0, pair, 1 - core).wait_recv()
        stage[2, pair] = ((dk_acc[seg] + part[0, pair]) * scale).astype(BF16)
        emit(2, pair, seg)
        part_copy(1, pair, 1 - core).wait_recv()
        stage[3, pair] = (dv_acc[seg] + part[1, pair]).astype(BF16)
        emit(3, pair, seg)
        return carry

    lax.fori_loop(0, chips, each_segment, 0)

    for a in range(4):
        ref = (o_ref, dq_ref, dk_ref, dv_ref)[a]
        for j in range(chips - 1):
            push_remote(a, j).wait_send()

        @pl.when(goes_to != core)
        def _():
            push_remote(a, chips - 1).wait_send()

        for pair in range(chips):
            seg = segment_of(pair, core)

            @pl.when(seg != me)
            def _():
                out_send_copy(a, pair, seg).wait_send()

            if a < 2:
                part_copy(a, pair, 1 - core).wait_send()
            spot = ref.at[:, pl.ds(pair * hd, hd)]
            pltpu.make_async_copy(spot, spot, out_recv.at[a, pair]).wait()


def by_heads(queries, keys, values, grad_out, retrieved, mem_bias):
    seq_count = lax.axis_size("seq")
    head_dev = lax.axis_size("head")
    seg_len, features = keys.shape
    heads = mem_bias.shape[0]
    hd = features // heads
    chips = seq_count // 2
    rows_dev, top = retrieved.shape
    seg_blocks = seg_len // BLK
    table = jnp.pad(retrieved.astype(F32), ((0, 8 - rows_dev), (0, 128 - top)))
    bias = jnp.stack([mem_bias * LOG2E, jnp.log1p(jnp.exp(mem_bias)) * LOG2E])
    dims = (seq_count, head_dev, chips, seg_len, hd, rows_dev, top)
    dma = pltpu.SemaphoreType.DMA
    vm = pltpu.VMEM
    anywhere = pl.BlockSpec(memory_space=pl.ANY)
    out = jax.ShapeDtypeStruct((seg_len, features), BF16)
    return pl.pallas_call(
        functools.partial(fused, dims),
        out_shape=(out,) * 4,
        in_specs=[
            pl.BlockSpec(memory_space=pltpu.VMEM),
            pl.BlockSpec(memory_space=pltpu.SMEM),
        ]
        + [anywhere] * 4,
        out_specs=(anywhere,) * 4,
        scratch_shapes=[
            vm((seq_count, head_dev, 8, 128), F32),
            vm((chips, seg_len, hd), BF16),
            vm((chips, seg_len, hd), BF16),
            vm((seq_count, seg_len, hd), BF16),
            vm((seq_count, seg_len, hd), BF16),
            vm((seq_count, hd, seg_len), BF16),
            vm((seq_count, hd, seg_len), BF16),
            vm((seq_count, seg_len, hd), F32),
            vm((seq_count, seg_len, hd), F32),
            vm((2, chips, seg_len, hd), F32),
            vm((4, chips, seg_len, hd), BF16),
            vm((seq_count * seg_blocks, seg_len), F32),
            vm((hd, seg_len), BF16),
            vm((hd, seg_len), BF16),
            vm((hd, seg_len), F32),
            vm((hd, seg_len), F32),
            vm((8, seg_len), F32),
            dma((head_dev - 1,)),
            dma((head_dev - 1,)),
            dma((seq_count - 1,)),
            dma((seq_count - 1,)),
            dma((4, chips)),
            dma((4, chips)),
            dma((2, chips)),
            dma((2, chips)),
            dma((2, chips)),
            dma((2, chips)),
            dma((4, chips)),
            dma((4, chips)),
        ],
        compiler_params=pltpu.CompilerParams(
            collective_id=0, has_side_effects=True, vmem_limit_bytes=56 * 1024 * 1024
        ),
    )(table, bias, queries, keys, values, grad_out)


def by_segments(queries, keys, values, grad_out, retrieved, mem_bias):
    seq_count = lax.axis_size("seq")
    position = lax.axis_index("seq")
    seg_len, features = keys.shape
    heads = mem_bias.shape[0]
    hd = features // heads
    seg_blocks = seg_len // BLK
    scale = 1.0 / math.sqrt(hd)
    lists = lax.all_gather(retrieved, "head", axis=0, tiled=True)
    all_keys = lax.all_gather(keys, "seq").reshape(seq_count, seg_len, heads, hd)
    all_values = lax.all_gather(values, "seq").reshape(seq_count, seg_len, heads, hd)
    q = queries.reshape(seg_len, heads, hd)
    g = grad_out.reshape(seg_len, heads, hd)
    row = jnp.arange(seg_len, dtype=jnp.int32)

    def score(k, key_seg):
        kb = k * seg_blocks + jnp.arange(seg_blocks, dtype=jnp.int32)
        block = position * seg_blocks + jnp.arange(seg_blocks, dtype=jnp.int32)
        named = jnp.any(lists[:, :, None] == kb[None, None, :], axis=1)
        named = named & (kb[None, :] < block[:, None])
        named = jnp.repeat(jnp.repeat(named, BLK, axis=0), BLK, axis=1)
        local = (k == position) & (row[None, :] <= row[:, None])
        bias = mem_bias[:, None, None]
        extra = jnp.where(
            local[None],
            jnp.where(named[None], jnp.log1p(jnp.exp(bias)), 0.0),
            jnp.where(named[None], bias, NEG),
        )
        return jnp.einsum("qhd,khd->hqk", q, key_seg, preferred_element_type=F32) * scale + extra

    def forward(carry, k):
        best, mass, acc = carry
        value = score(k, all_keys[k])
        new = jnp.maximum(best, jnp.max(value, axis=-1, keepdims=True))
        shrink = jnp.exp(best - new)
        weight = jnp.where(value > 0.5 * NEG, jnp.exp(value - new), 0.0)
        acc = acc * shrink + jnp.einsum(
            "hqk,khd->hqd", weight.astype(BF16), all_values[k], preferred_element_type=F32
        )
        return (new, mass * shrink + jnp.sum(weight, axis=-1, keepdims=True), acc), None

    start = (
        jnp.full((heads, seg_len, 1), NEG, F32),
        jnp.zeros((heads, seg_len, 1), F32),
        jnp.zeros((heads, seg_len, hd), F32),
    )
    order = jnp.arange(seq_count, dtype=jnp.int32)
    (best, mass, acc), _ = lax.scan(forward, start, order)
    attended = acc / mass
    lse = best + jnp.log(mass)
    delta = jnp.sum(attended * g.astype(F32).transpose(1, 0, 2), axis=-1, keepdims=True)

    def backward(dq, k):
        prob = jnp.exp(score(k, all_keys[k]) - lse)
        dprob = jnp.einsum("qhd,khd->hqk", g, all_values[k], preferred_element_type=F32)
        dscore = (prob * (dprob - delta) * scale).astype(BF16)
        dq = dq + jnp.einsum("hqk,khd->hqd", dscore, all_keys[k], preferred_element_type=F32)
        dk = jnp.einsum("hqk,qhd->khd", dscore, q, preferred_element_type=F32)
        dv = jnp.einsum("hqk,qhd->khd", prob.astype(BF16), g, preferred_element_type=F32)
        return dq, (dk.reshape(seg_len, features), dv.reshape(seg_len, features))

    dq, (dk, dv) = lax.scan(backward, jnp.zeros((heads, seg_len, hd), F32), order)
    dk = lax.psum_scatter(dk, "seq", scatter_dimension=0)
    dv = lax.psum_scatter(dv, "seq", scatter_dimension=0)

    def rows(x):
        return x.transpose(1, 0, 2).reshape(seg_len, features).astype(BF16)

    return rows(attended), rows(dq), dk.astype(BF16), dv.astype(BF16)


def shards(queries, keys, values, grad_out, retrieved, mem_bias):
    heads = mem_bias.shape[0]
    hd = keys.shape[1] // heads
    if (
        lax.axis_size("seq") == 2 * heads
        and hd % 128 == 0
        and retrieved.shape[0] <= 8
        and heads > 1
        and lax.axis_size("head") > 1
    ):
        return by_heads(queries, keys, values, grad_out, retrieved, mem_bias)
    return by_segments(queries, keys, values, grad_out, retrieved, mem_bias)


def solution(mesh):
    placed = (
        P("seq", "head"),
        P("seq", "head"),
        P("seq", "head"),
        P("seq", "head"),
        P(("seq", "head"), None),
        P("head"),
    )
    return jax.shard_map(
        shards,
        mesh=mesh,
        in_specs=placed,
        out_specs=(P("seq", "head"), P("seq", "head"), P("seq", "head"), P("seq", "head")),
        check_vma=False,
    )
```

time: 368 us -> 99.2 us (0.27); the launches traced: 361 us -> 98.9 us
  local copies, waits for them, and re-layouts: 137 us -> 5.78 us
  other arithmetic: 129 us -> 1.28 us
  Pallas kernels: 0 us -> 91.2 us
  matrix products: 47.7 us -> 0 us
  blocking collectives: 21.8 us -> 0 us
  starting transfers between devices: 17.6 us -> 0 us
  waiting for transfers between devices: 7.64 us -> 0 us
    pallas_call x0 -> x1, Pallas kernels: none -> 91.2 us  [by_heads(): pl.pallas_call(functools.partial(fused, dims), out_shape=(out,) * 4, in_s...]
    scatter-add x4 -> x0, other arithmetic: 90.6 us -> none  [the longest x1 38.9 us: step(): tile_kgrad.at[slot_rows]]
    reshape x13 -> x0, local copies, waits for them, and re-layouts: 74.8 us -> none  [the longest x1 19.9 us: step(): results[4].reshape(group_blocks * TOPK, BLK, features)]
    dot_general x10 -> x0, matrix products: 43.3 us -> none  [product(): jnp.einsum(pattern, former, latter, preferred_element_type=jnp.float32)]
    convert_element_type x9 -> x1, other arithmetic: 27.4 us -> 0.69 us  [by_heads(): table = jnp.pad(retrieved.astype(F32), ((0, 8 - rows_dev), (0, 128 - top)))]
    transpose x4 -> x0, local copies, waits for them, and re-layouts: 25.9 us -> none  [product(): jnp.einsum(pattern, former, latter, preferred_element_type=jnp.float32)]
    all_gather x2 -> x0, blocking collectives: 21.8 us -> none  [the longest x1 12.8 us: shards(): named_blocks = lax.all_gather(retrieved, 'head', axis=0, tiled=True)]
    gather x4 -> x0, local copies, waits for them, and re-layouts: 19.9 us -> none  [the longest x1 8.14 us: step(): tile_values[slot_rows].reshape(group_blocks, TOPK, BLK, features)]
  transfers between devices with their start and end apart: 4 -> 0, of which waited for: 1 -> 0; matrix products, arithmetic and copies ran while one was open for 47% -> 0% of each run, Pallas kernels for 0% -> 0%
where the time goes in v1:
time: 99.2 us; the launch traced here: 98.9 us
  Pallas kernels  91.2 us (92%)
  local copies, waits for them, and re-layouts  5.78 us (6%)
  other arithmetic  1.28 us (1%)
    pallas_call x1, Pallas kernels, by_heads(): pl.pallas_call(functools.partial(fused, dims), out_shape=(out,) * 4, in_s...  91.2 us
    unnamed x12, local copies, waits for them, and re-layouts  5.19 us

profile of v1, /device:TPU:0, one launch (start us, length us, event | category | flops | bytes accessed | tf_op | source)
XLA Modules:
  0.0 98.9 jit_solution(8445448165918801322)
XLA Ops:
  0.6 0.0 copy-start.3
  0.6 0.7 convert_element_type.5
  1.3 0.0 copy-done.3
  1.3 0.6 pad_maximum_fusion.bias_ref
  1.9 0.6 pad.4.table_in
  2.5 91.2 %shard_map.93 = (bf16[512,512]{1,0:T(8,128)(2,1)}, bf16[512,512]{1,0:T(8,128)(2,1)}, bf16[512,512]{1,0:T(8,128)(2,1)}, bf16[512,512]{1,0:T(8,128)(2,1)}) custom-call(f32[8,128]{1,0:T(8,128)} %pad.4.table_in, f32[2,4]{1,0:T(2,128)} %pad_maximum_fusion.bias_ref, bf16[512,512]{1,0:T(8,128)(2,1)} %q_ref.1, bf16[512,512]{1,0:T(8,128)(2,1)} %k_ref.1, ...), custom_call_target="tpu_custom_call" | custom-call | tf_op jit(solution)/shard_map/pallas_call | solution.py:383
  93.7 0.0 copy-start.2
  93.7 1.9 %copy.14 = bf16[512,512]{1,0:T(8,128)(2,1)} copy(bf16[512,512]{1,0:T(8,128)(2,1)} %get-tuple-element.10) | data formatting | bytes 1048576
  95.6 0.0 copy-done.2
  95.6 0.0 copy-start.1
  95.6 0.8 copy.15
  96.4 0.4 copy-done.1
  96.9 0.0 copy-start
  96.9 0.8 copy.16
  97.7 0.4 copy-done
  98.1 0.8 copy.17
  (1 shorter events, 0.0 us)
Async XLA Ops:
  0.6 0.7 copy-start.3
  93.7 1.9 %copy-start.2 = (bf16[512,512]{1,0:T(8,128)(2,1)S(1)}, bf16[512,512]{1,0:T(8,128)(2,1)}, u32[]{:S(2)}) copy-start(bf16[512,512]{1,0:T(8,128)(2,1)} %get-tuple-element.11) | copy-start | bytes 1572868
  95.6 1.2 %copy-start.1 = (bf16[512,512]{1,0:T(8,128)(2,1)S(1)}, bf16[512,512]{1,0:T(8,128)(2,1)}, u32[]{:S(2)}) copy-start(bf16[512,512]{1,0:T(8,128)(2,1)} %get-tuple-element.12) | copy-start | bytes 1572868
  96.9 1.2 %copy-start = (bf16[512,512]{1,0:T(8,128)(2,1)S(1)}, bf16[512,512]{1,0:T(8,128)(2,1)}, u32[]{:S(2)}) copy-start(bf16[512,512]{1,0:T(8,128)(2,1)} %get-tuple-element.13) | copy-start | bytes 1572868

commit v2 on v1

--- a/solution.py
+++ b/solution.py
@@ -75,6 +75,9 @@
     core = lax.rem(me, 2)
     sibling = chip * 2 + 1 - core
 
+    table[me, zed] = jnp.zeros((8, 128), F32)
+    table[me, zed, 0:rows_dev, 0:top] = table_in[...].astype(F32)
+
     barrier = pltpu.get_barrier_semaphore()
     for j in range(1, seq_count):
         pl.semaphore_signal(
@@ -88,7 +91,7 @@
 
     def hop1(j):
         return pltpu.make_async_remote_copy(
-            src_ref=table_in,
+            src_ref=table.at[me, zed],
             dst_ref=table.at[me, zed],
             send_sem=hop1_send.at[j - 1],
             recv_sem=hop1_recv.at[j - 1],
@@ -98,7 +101,6 @@
 
     for j in range(1, head_dev):
         hop1(j).start()
-    table[me, zed] = table_in[...]
 
     arrays = ((k_ref, k_buf), (q_ref, q_buf), (v_ref, v_buf), (g_ref, g_buf))
     goes_to = owner_core(me)
@@ -158,6 +160,7 @@
 
     dk_acc[...] = jnp.zeros_like(dk_acc)
     dv_acc[...] = jnp.zeros_like(dv_acc)
+    dqt[...] = jnp.zeros_like(dqt)
 
     def segment_of(pair, which):
         return pair * 2 + lax.rem(pair + which, 2)
@@ -183,7 +186,8 @@
         for pair in range(chips):
             in_wait(2 * kind, pair)
             forward(kind, pair, core).start()
-            in_wait(2 * kind + 1, pair)
+            if kind == 0:
+                in_wait(1, pair)
     for j in range(1, seq_count):
         hop2(j).wait()
     for pair in range(chips):
@@ -195,14 +199,15 @@
             turned[other] = buf[other].T
             forward(kind, pair, core).wait_send()
 
-    bias2 = bias_ref[0, chip]
-    both2 = bias_ref[1, chip]
+    bias_row = jnp.full((1, seg_len), bias_ref[0, chip], F32)
+    bias2 = bias_row * LOG2E
+    both2 = jnp.log(1.0 + jnp.exp(bias_row)) * LOG2E
     score2 = scale * LOG2E
     kb_seg = (seg_blocks, 1, seg_len)
     tile = (seg_blocks, BLK, seg_len)
 
-    def scores(k, rows):
-        raw = matmul(k_buf[k], qt[...]).reshape(tile)
+    def scores(k, rows, pair):
+        raw = matmul(k_buf[k], qt[pair]).reshape(tile)
         return raw * score2 + rows.reshape(kb_seg)
 
     def triangle(value):
@@ -210,8 +215,8 @@
         query = lax.broadcasted_iota(jnp.int32, (seg_len, seg_len), 1)
         return jnp.where((key <= query).reshape(tile), value, NEG)
 
-    def rows_of(k):
-        return bias_rows[pl.ds(pl.multiple_of(k * seg_blocks, seg_blocks), seg_blocks), :]
+    def rows_of(k, pair):
+        return bias_rows[pair, pl.ds(pl.multiple_of(k * seg_blocks, seg_blocks), seg_blocks), :]
 
     def out_send_copy(a, pair, seg):
         ref = (o_ref, dq_ref, dk_ref, dv_ref)[a]
@@ -249,8 +254,11 @@
             device_id_type=MESH,
         )
 
-    def each_segment(step, carry):
-        pair = chips - 1 - step
+    def turn(step):
+        return lax.rem(chip + 1 + step, chips)
+
+    def forward_segment(step, carry):
+        pair = turn(step)
         seg = segment_of(pair, core)
         lists = table[seg].reshape(head_dev * 8, 128).astype(BF16)
         slot = lax.broadcasted_iota(jnp.int32, (head_dev * 8, seg_len), 0)
@@ -273,64 +281,83 @@
         before = jnp.where(
             same, jnp.where(named, both2, 0.0), jnp.where(named, bias2, NEG)
         )
-        bias_rows[...] = jnp.where(kb < block, before, jnp.where(kb == block, 0.0, NEG))
-
-        qt[...] = q_buf[pair].T
-        gt[...] = g_buf[pair].T
-
-        first = triangle(scores(seg, rows_of(seg)))
+        bias_rows[pair] = jnp.where(kb < block, before, jnp.where(kb == block, 0.0, NEG))
+
+        qt[pair] = q_buf[pair].T
+
+        first = triangle(scores(seg, rows_of(seg, pair), pair))
         top_row = jnp.max(jnp.max(first, axis=0), axis=0, keepdims=True)
         weight = jnp.exp2(first - top_row.reshape(1, 1, seg_len))
-        stat[0:1, :] = top_row
-        stat[1:2, :] = jnp.sum(jnp.sum(weight, axis=0), axis=0, keepdims=True)
-        ot[...] = matmul(vt_buf[seg], weight.reshape(seg_len, seg_len).astype(BF16))
+        stat[pair, 0:1, :] = top_row
+        stat[pair, 1:2, :] = jnp.sum(jnp.sum(weight, axis=0), axis=0, keepdims=True)
+        ot[pair] = matmul(vt_buf[seg], weight.reshape(seg_len, seg_len).astype(BF16))
 
         def forward_tile(k, c):
-            value = scores(k, rows_of(k))
-            old = stat[0:1, :]
+            value = scores(k, rows_of(k, pair), pair)
+            old = stat[pair, 0:1, :]
             new = jnp.maximum(old, jnp.max(jnp.max(value, axis=0), axis=0, keepdims=True))
             shrink = jnp.exp2(old - new)
             weight = jnp.exp2(value - new.reshape(1, 1, seg_len))
-            stat[0:1, :] = new
-            stat[1:2, :] = stat[1:2, :] * shrink + jnp.sum(
+            stat[pair, 0:1, :] = new
+            stat[pair, 1:2, :] = stat[pair, 1:2, :] * shrink + jnp.sum(
                 jnp.sum(weight, axis=0), axis=0, keepdims=True
             )
-            ot[...] = ot[...] * shrink + matmul(
+            ot[pair] = ot[pair] * shrink + matmul(
                 vt_buf[k], weight.reshape(seg_len, seg_len).astype(BF16)
             )
             return c
 
         lax.fori_loop(0, seg, forward_tile, 0)
-        mass = stat[1:2, :]
-        ot[...] = ot[...] / mass
-        stage[0, pair] = ot[...].T.astype(BF16)
+        mass = stat[pair, 1:2, :]
+        ot[pair] = ot[pair] / mass
+        stage[0, pair] = ot[pair].T.astype(BF16)
         emit(0, pair, seg)
-        lse = stat[0:1, :] + jnp.log2(mass)
-        stat[2:3, :] = jnp.sum(ot[...] * gt[...].astype(F32), axis=0, keepdims=True)
-        stat[3:4, :] = lse
-        dqt[...] = jnp.zeros_like(dqt)
-
-        def backward_tile(k, diagonal):
-            value = scores(k, rows_of(k) - stat[3:4, :])
-            if diagonal:
-                value = triangle(value)
-            prob = jnp.exp2(value).reshape(seg_len, seg_len)
-            dprob = matmul(v_buf[k], gt[...])
-            dscore = (prob * (dprob - stat[2:3, :])).astype(BF16)
-            dv_acc[k] += matmul(prob.astype(BF16), g_buf[pair])
-            dk_acc[k] += matmul(dscore, q_buf[pair])
-            dqt[...] += matmul(kt_buf[k], dscore)
-
-        backward_tile(seg, True)
-
-        def backward_step(k, c):
-            backward_tile(k, False)
+        stat[pair, 3:4, :] = stat[pair, 0:1, :] + jnp.log2(mass)
+        return carry
+
+    lax.fori_loop(0, chips, forward_segment, 0)
+
+    for pair in range(chips):
+        in_wait(3, pair)
+        gt[pair] = g_buf[pair].T
+        stat[pair, 2:3, :] = jnp.sum(ot[pair] * gt[pair].astype(F32), axis=0, keepdims=True)
+
+    def backward_tile(k, pair, diagonal):
+        value = scores(k, rows_of(k, pair) - stat[pair, 3:4, :], pair)
+        if diagonal:
+            value = triangle(value)
+        prob = jnp.exp2(value).reshape(seg_len, seg_len)
+        dprob = matmul(v_buf[k], gt[pair])
+        dscore = (prob * (dprob - stat[pair, 2:3, :])).astype(BF16)
+        dv_acc[k] += matmul(prob.astype(BF16), g_buf[pair])
+        dk_acc[k] += matmul(dscore, q_buf[pair])
+        dqt[pair] += matmul(kt_buf[k], dscore)
+
+    def finish_pair(step, carry):
+        pair = turn(step)
+        seg = segment_of(pair, core)
+
+        def visit(index, c):
+            other = index // 2
+            query_pair = jnp.maximum(pair, other)
+            k = jnp.minimum(pair, other) * 2 + lax.rem(index, 2)
+            query_seg = segment_of(query_pair, core)
+            live = lax.rem(other - chip - 1 + chips, chips) >= step
+
+            @pl.when(live & (k < query_seg))
+            def _():
+                backward_tile(k, query_pair, False)
+
+            @pl.when(live & (k == query_seg))
+            def _():
+                backward_tile(k, query_pair, True)
+
             return c
 
-        lax.fori_loop(0, seg, backward_step, 0)
+        lax.fori_loop(0, 2 * chips, visit, 0)
         part_copy(0, pair, 1 - core).start()
         part_copy(1, pair, 1 - core).start()
-        stage[1, pair] = (dqt[...] * scale).T.astype(BF16)
+        stage[1, pair] = (dqt[pair] * scale).T.astype(BF16)
         emit(1, pair, seg)
         part_copy(0, pair, 1 - core).wait_recv()
         stage[2, pair] = ((dk_acc[seg] + part[0, pair]) * scale).astype(BF16)
@@ -340,7 +367,7 @@
         emit(3, pair, seg)
         return carry
 
-    lax.fori_loop(0, chips, each_segment, 0)
+    lax.fori_loop(0, chips, finish_pair, 0)
 
     for a in range(4):
         ref = (o_ref, dq_ref, dk_ref, dv_ref)[a]
@@ -373,8 +400,6 @@
     chips = seq_count // 2
     rows_dev, top = retrieved.shape
     seg_blocks = seg_len // BLK
-    table = jnp.pad(retrieved.astype(F32), ((0, 8 - rows_dev), (0, 128 - top)))
-    bias = jnp.stack([mem_bias * LOG2E, jnp.log1p(jnp.exp(mem_bias)) * LOG2E])
     dims = (seq_count, head_dev, chips, seg_len, hd, rows_dev, top)
     dma = pltpu.SemaphoreType.DMA
     vm = pltpu.VMEM
@@ -401,12 +426,12 @@
             vm((seq_count, seg_len, hd), F32),
             vm((2, chips, seg_len, hd), F32),
             vm((4, chips, seg_len, hd), BF16),
-            vm((seq_count * seg_blocks, seg_len), F32),
-            vm((hd, seg_len), BF16),
-            vm((hd, seg_len), BF16),
-            vm((hd, seg_len), F32),
-            vm((hd, seg_len), F32),
-            vm((8, seg_len), F32),
+            vm((chips, seq_count * seg_blocks, seg_len), F32),
+            vm((chips, hd, seg_len), BF16),
+            vm((chips, hd, seg_len), BF16),
+            vm((chips, hd, seg_len), F32),
+            vm((chips, hd, seg_len), F32),
+            vm((chips, 8, seg_len), F32),
             dma((head_dev - 1,)),
             dma((head_dev - 1,)),
             dma((seq_count - 1,)),
@@ -423,7 +448,7 @@
         compiler_params=pltpu.CompilerParams(
             collective_id=0, has_side_effects=True, vmem_limit_bytes=56 * 1024 * 1024
         ),
-    )(table, bias, queries, keys, values, grad_out)
+    )(retrieved, mem_bias.reshape(1, heads), queries, keys, values, grad_out)
 
 
 def by_segments(queries, keys, values, grad_out, retrieved, mem_bias):

time: 99.2 us -> 83.1 us (0.84); the launches traced: 98.9 us -> 81.5 us
  Pallas kernels: 91.2 us -> 75.7 us
  other arithmetic: 1.28 us -> 0 us
    pallas_call x1, Pallas kernels: 91.2 us -> 75.7 us  [by_heads(): pl.pallas_call(functools.partial(fused, dims), out_shape=(out,) * 4, in_s...]
    unnamed x12 -> x10, local copies, waits for them, and re-layouts: 5.19 us -> 5.18 us
where the time goes in v2:
time: 83.1 us; the launch traced here: 81.5 us
  Pallas kernels  75.7 us (91%)
  local copies, waits for them, and re-layouts  5.18 us (6%)
    pallas_call x1, Pallas kernels, by_heads(): pl.pallas_call(functools.partial(fused, dims), out_shape=(out,) * 4, in_s...  75.7 us
    unnamed x10, local copies, waits for them, and re-layouts  5.18 us

profile of v2, /device:TPU:0, one launch (start us, length us, event | category | flops | bytes accessed | tf_op | source)
XLA Modules:
  0.0 81.5 jit_solution(17297925404146571666)
XLA Ops:
  0.6 75.7 %shard_map.93 = (bf16[512,512]{1,0:T(8,128)(2,1)}, bf16[512,512]{1,0:T(8,128)(2,1)}, bf16[512,512]{1,0:T(8,128)(2,1)}, bf16[512,512]{1,0:T(8,128)(2,1)}) custom-call(s32[2,16]{1,0:T(2,128)} %table_in.1, f32[1,4]{1,0:T(1,128)} %bitcast.1, bf16[512,512]{1,0:T(8,128)(2,1)} %q_ref.1, bf16[512,512]{1,0:T(8,128)(2,1)} %k_ref.1, bf16[512,512]{1,0:T(8,128)(2,1)} %v_ref.1, ...), custom_call_target="tpu_custom_call" | custom-call | tf_op jit(solution)/shard_map/pallas_call | solution.py:408
  76.3 0.0 copy-start.2
  76.3 1.9 %copy.14 = bf16[512,512]{1,0:T(8,128)(2,1)} copy(bf16[512,512]{1,0:T(8,128)(2,1)} %get-tuple-element.8) | data formatting | bytes 1048576
  78.2 0.0 copy-done.2
  78.2 0.0 copy-start.1
  78.2 0.8 copy.15
  79.0 0.4 copy-done.1
  79.5 0.0 copy-start
  79.5 0.8 copy.16
  80.3 0.4 copy-done
  80.7 0.8 copy.17
Async XLA Ops:
  76.3 1.9 %copy-start.2 = (bf16[512,512]{1,0:T(8,128)(2,1)S(1)}, bf16[512,512]{1,0:T(8,128)(2,1)}, u32[]{:S(2)}) copy-start(bf16[512,512]{1,0:T(8,128)(2,1)} %get-tuple-element.9) | copy-start | bytes 1572868
  78.2 1.2 %copy-start.1 = (bf16[512,512]{1,0:T(8,128)(2,1)S(1)}, bf16[512,512]{1,0:T(8,128)(2,1)}, u32[]{:S(2)}) copy-start(bf16[512,512]{1,0:T(8,128)(2,1)} %get-tuple-element.10) | copy-start | bytes 1572868
  79.5 1.2 %copy-start = (bf16[512,512]{1,0:T(8,128)(2,1)S(1)}, bf16[512,512]{1,0:T(8,128)(2,1)}, u32[]{:S(2)}) copy-start(bf16[512,512]{1,0:T(8,128)(2,1)} %get-tuple-element.11) | copy-start | bytes 1572868
